TPU v7x, 32 devices: a whole 2x2x4 slice. The times are simulated.
32 devices in a mesh: var: 4 (over z), own: 4 (over y, x), sub: 2 (over core).
Axes of the slice: x: 2, y: 2, z: 4, core: 2. Of those that a mesh axis runs over, the one named last changes fastest.
Arguments:
- capacity_blocks: bfloat16 [2048, 5, 128, 128], P(('var', 'own', 'sub')), may hold values from -0.078125 to 0.078125
- capacity_rows: int32 [2048, 5], P(('var', 'own', 'sub')), may hold values from 0 to 7, all different within a row
- cover_self: bfloat16 [2048, 128, 128], P(('var', 'own', 'sub')), may hold values from -0.5 to 0.5
- cover_prev: bfloat16 [2048, 128, 128], P(('var', 'own', 'sub')), may hold values from -0.5 to 0.5
- scaling: bfloat16 [2048, 128], P(('var', 'own', 'sub')), may hold values from 0.099609375 to 10
Outputs:
- cover_diag: bfloat16 [2048, 128, 128], P(('var', 'own', 'sub'))
- cover_lower: bfloat16 [2048, 128, 128], P(('var', 'own', 'sub'))
- capacity_normal: float32 [1024, 1024], P(('var', 'own', 'sub'))
Inputs may be any that keep to these rules, and one draw needn't show every extreme that they name: `capacity_rows`: each column block names 5 different capacity row blocks, and every capacity row block is named somewhere.
All inputs are finite; a program needn't handle non-finite values.
Results may differ from a plain program's by a relative error of at most 0.0049.
Values may be sent and summed in bfloat16 or wider, within the bound.
No kernel may reach another device: no remote copies, remote signals or barrier semaphores. Data moves between devices by JAX's collectives and lax.ppermute only.
A program may use at most 192 MiB of HBM per device.

v0:
```python
import math

import jax
import jax.numpy as jnp
from jax import lax
from jax.sharding import PartitionSpec as P

CAP = 8


def shifted(value, axis, steps):
    count = lax.axis_size(axis)
    initial, last = (max(0, -steps), min(count, count - steps))
    return lax.ppermute(value, axis, [(source, source + steps) for source in range(initial, last)])


def accumulate(partial_value, inputs):
    blocks, row_ids, scale_row = inputs
    scaled = (blocks.astype(jnp.float32) * scale_row.astype(jnp.float32)[:, None, None, :]).astype(
        jnp.bfloat16
    )
    tile_sums = jnp.einsum("kpiv,kqjv->kpqij", scaled, blocks, preferred_element_type=jnp.float32)
    per_block = row_ids.shape[1]
    left_rows = jnp.broadcast_to(
        row_ids[:, :, None], (row_ids.shape[0], per_block, per_block)
    ).reshape(-1)
    right_rows = jnp.broadcast_to(
        row_ids[:, None, :], (row_ids.shape[0], per_block, per_block)
    ).reshape(-1)
    edge_size = blocks.shape[-1]
    partial_value = partial_value.at[left_rows, :, right_rows, :].add(
        tile_sums.reshape(-1, edge_size, edge_size)
    )
    return (partial_value, None)


def body(capacity_blocks, capacity_rows, cover_self, cover_prev, scaling):
    edge_size = capacity_blocks.shape[-1]
    local_blocks = capacity_blocks.shape[0]
    received = shifted((cover_self[-1:], scaling[-1:]), ("var", "own", "sub"), 1)
    group_size = math.gcd(local_blocks, 16)
    turns = local_blocks // group_size
    inputs = (
        capacity_blocks.reshape((turns, group_size) + capacity_blocks.shape[1:]),
        capacity_rows.reshape(turns, group_size, -1),
        scaling.reshape(turns, group_size, -1),
    )
    start = jnp.zeros((CAP, edge_size, CAP, edge_size), jnp.float32)
    result, unused = lax.scan(accumulate, start, inputs)
    full_rows = CAP * edge_size
    flat_sum = result.reshape(full_rows, full_rows)
    capacity_normal = lax.psum_scatter(
        flat_sum, ("var", "own", "sub"), scatter_dimension=0, tiled=True
    )
    self_prev = jnp.concatenate([received[0], cover_self[:-1]], axis=0)
    scale_prev = jnp.concatenate([received[1], scaling[:-1]], axis=0)
    scaled_self = (cover_self.astype(jnp.float32) * scaling.astype(jnp.float32)[:, None, :]).astype(
        jnp.bfloat16
    )
    scaled_prev = (
        cover_prev.astype(jnp.float32) * scale_prev.astype(jnp.float32)[:, None, :]
    ).astype(jnp.bfloat16)
    diag_sum = jnp.einsum(
        "kiv,kjv->kij", scaled_self, cover_self, preferred_element_type=jnp.float32
    )
    diag_sum = diag_sum + jnp.einsum(
        "kiv,kjv->kij", scaled_prev, cover_prev, preferred_element_type=jnp.float32
    )
    lower_sum = jnp.einsum(
        "kiv,kjv->kij", scaled_prev, self_prev, preferred_element_type=jnp.float32
    )
    return (diag_sum.astype(jnp.bfloat16), lower_sum.astype(jnp.bfloat16), capacity_normal)


def solution(mesh):
    placed = (
        P(("var", "own", "sub"), None, None, None),
        P(("var", "own", "sub"), None),
        P(("var", "own", "sub"), None, None),
        P(("var", "own", "sub"), None, None),
        P(("var", "own", "sub"), None),
    )
    return jax.shard_map(
        body,
        mesh=mesh,
        in_specs=placed,
        out_specs=(
            P(("var", "own", "sub"), None, None),
            P(("var", "own", "sub"), None, None),
            P(("var", "own", "sub"), None),
        ),
        check_vma=False,
    )
```

profile of v0, /device:TPU:0, one launch (start us, length us, event | category | flops | bytes accessed | tf_op | source)
XLA Modules:
  0.0 681.6 jit_solution(1926998110981631207)
XLA Ops:
  7.2 0.0 copy-start.2
  7.2 0.0 reduce-scatter.2.cloned.1.call-start
  7.2 0.8 reshape.110
  8.0 2.5 broadcast_in_dim.8
  10.4 0.0 copy-done.2
  10.4 512.4 %while.10 = (s32[]{:T(128)}, f32[8,128,8,128]{3,1,2,0:T(8,128)}, s32[4,16,5]{1,0,2:T(4,128)S(1)}, bf16[4,16,5,128,128]{4,3,2,1,0:T(8,128)(2,1)}, bf16[4,16,128]{2,1,0:T(8,128)(2,1)S(1)}, /*index=5*/s32[]{:T(128)}) while((s32[]{:T(128)}, f32[8,128,8,128]{3,1,2,0:T(8,128)}, s32[4,16,5]{1,0,2:T(4,128)S(1)}, ...), condition=%wide.region_2.3_spmd, body=%wide.region_0.2_spmd.sunk | while | flops 1688215424 | bytes 162570400 | solution.py:49
  10.5 0.1 copy.25
  10.6 0.2 reshape.130
  10.7 0.1 broadcast_in_dim.11
  10.8 0.2 reshape.129
  11.0 14.8 %convolution_bitcast_fusion.2 = f32[16,5,5,128,128]{3,4,1,2,0:T(8,128)} fusion(f32[16,128]{1,0:T(8,128)S(1)} %bitcast_convert_fusion.2, bf16[4,16,5,128,128]{4,3,2,1,0:T(8,128)(2,1)} %get-tuple-element.92, s32[]{:T(128)S(6)} %copy.30), kind=kOutput, calls=%fused_computation.1.clone.1 | convolution fusion | flops 1681653760 | bytes 31466496 | tf_op jit(solution)/shard_map/while/body/eval_jaxpr/kpiv,kqjv->kpqij/dot_general | solution.py:22
  25.7 27.4 %copy.26 = f32[16,5,5,128,128]{4,3,2,1,0:T(8,128)} copy(f32[16,5,5,128,128]{3,4,1,2,0:T(8,128)} %convolution_bitcast_fusion.2) | data formatting | bytes 52428800 | tf_op jit(solution)/shard_map/while/body/eval_jaxpr/kpiv,kqjv->kpqij/transpose | solution.py:22
  53.1 85.4 %scatter_fusion = f32[8,128,8,128]{3,1,2,0:T(8,128)} fusion(f32[8,128,8,128]{3,1,2,0:T(8,128)} %get-tuple-element.84, s32[400]{0:T(512)S(1)} %bitcast.53, f32[400,128,128]{2,1,0:T(8,128)} %bitcast.52), kind=kCustom, calls=%fused_computation.clone.1 | custom fusion | flops 6553600 | bytes 78646400 | tf_op jit(solution)/shard_map/while/body/eval_jaxpr/scatter-add | solution.py:31
  138.5 0.1 copy.25
  138.6 0.2 reshape.130
  138.7 0.1 broadcast_in_dim.11
  138.8 0.2 reshape.129
  139.0 14.8 %convolution_bitcast_fusion.2 = f32[16,5,5,128,128]{3,4,1,2,0:T(8,128)} fusion(f32[16,128]{1,0:T(8,128)S(1)} %bitcast_convert_fusion.2, bf16[4,16,5,128,128]{4,3,2,1,0:T(8,128)(2,1)} %get-tuple-element.92, s32[]{:T(128)S(6)} %copy.30), kind=kOutput, calls=%fused_computation.1.clone.1 | convolution fusion | flops 1681653760 | bytes 31466496 | tf_op jit(solution)/shard_map/while/body/eval_jaxpr/kpiv,kqjv->kpqij/dot_general | solution.py:22
  153.8 27.4 %copy.26 = f32[16,5,5,128,128]{4,3,2,1,0:T(8,128)} copy(f32[16,5,5,128,128]{3,4,1,2,0:T(8,128)} %convolution_bitcast_fusion.2) | data formatting | bytes 52428800 | tf_op jit(solution)/shard_map/while/body/eval_jaxpr/kpiv,kqjv->kpqij/transpose | solution.py:22
  181.1 85.5 %scatter_fusion = f32[8,128,8,128]{3,1,2,0:T(8,128)} fusion(f32[8,128,8,128]{3,1,2,0:T(8,128)} %get-tuple-element.84, s32[400]{0:T(512)S(1)} %bitcast.53, f32[400,128,128]{2,1,0:T(8,128)} %bitcast.52), kind=kCustom, calls=%fused_computation.clone.1 | custom fusion | flops 6553600 | bytes 78646400 | tf_op jit(solution)/shard_map/while/body/eval_jaxpr/scatter-add | solution.py:31
  266.6 0.1 copy.25
  266.7 0.2 reshape.130
  266.9 0.1 broadcast_in_dim.11
  266.9 0.2 reshape.129
  267.1 14.8 %convolution_bitcast_fusion.2 = f32[16,5,5,128,128]{3,4,1,2,0:T(8,128)} fusion(f32[16,128]{1,0:T(8,128)S(1)} %bitcast_convert_fusion.2, bf16[4,16,5,128,128]{4,3,2,1,0:T(8,128)(2,1)} %get-tuple-element.92, s32[]{:T(128)S(6)} %copy.30), kind=kOutput, calls=%fused_computation.1.clone.1 | convolution fusion | flops 1681653760 | bytes 31466496 | tf_op jit(solution)/shard_map/while/body/eval_jaxpr/kpiv,kqjv->kpqij/dot_general | solution.py:22
  281.9 27.4 %copy.26 = f32[16,5,5,128,128]{4,3,2,1,0:T(8,128)} copy(f32[16,5,5,128,128]{3,4,1,2,0:T(8,128)} %convolution_bitcast_fusion.2) | data formatting | bytes 52428800 | tf_op jit(solution)/shard_map/while/body/eval_jaxpr/kpiv,kqjv->kpqij/transpose | solution.py:22
  309.3 85.4 %scatter_fusion = f32[8,128,8,128]{3,1,2,0:T(8,128)} fusion(f32[8,128,8,128]{3,1,2,0:T(8,128)} %get-tuple-element.84, s32[400]{0:T(512)S(1)} %bitcast.53, f32[400,128,128]{2,1,0:T(8,128)} %bitcast.52), kind=kCustom, calls=%fused_computation.clone.1 | custom fusion | flops 6553600 | bytes 78646400 | tf_op jit(solution)/shard_map/while/body/eval_jaxpr/scatter-add | solution.py:31
  394.7 0.1 copy.25
  394.8 0.2 reshape.130
  395.0 0.1 broadcast_in_dim.11
  395.1 0.2 reshape.129
  395.3 14.8 %convolution_bitcast_fusion.2 = f32[16,5,5,128,128]{3,4,1,2,0:T(8,128)} fusion(f32[16,128]{1,0:T(8,128)S(1)} %bitcast_convert_fusion.2, bf16[4,16,5,128,128]{4,3,2,1,0:T(8,128)(2,1)} %get-tuple-element.92, s32[]{:T(128)S(6)} %copy.30), kind=kOutput, calls=%fused_computation.1.clone.1 | convolution fusion | flops 1681653760 | bytes 31466496 | tf_op jit(solution)/shard_map/while/body/eval_jaxpr/kpiv,kqjv->kpqij/dot_general | solution.py:22
  410.0 27.4 %copy.26 = f32[16,5,5,128,128]{4,3,2,1,0:T(8,128)} copy(f32[16,5,5,128,128]{3,4,1,2,0:T(8,128)} %convolution_bitcast_fusion.2) | data formatting | bytes 52428800 | tf_op jit(solution)/shard_map/while/body/eval_jaxpr/kpiv,kqjv->kpqij/transpose | solution.py:22
  437.4 85.4 %scatter_fusion = f32[8,128,8,128]{3,1,2,0:T(8,128)} fusion(f32[8,128,8,128]{3,1,2,0:T(8,128)} %get-tuple-element.84, s32[400]{0:T(512)S(1)} %bitcast.53, f32[400,128,128]{2,1,0:T(8,128)} %bitcast.52), kind=kCustom, calls=%fused_computation.clone.1 | custom fusion | flops 6553600 | bytes 78646400 | tf_op jit(solution)/shard_map/while/body/eval_jaxpr/scatter-add | solution.py:31
  522.8 4.6 copy.15
  527.4 2.9 copy.22
  530.3 0.0 copy-start
  530.3 0.0 reduce-scatter.2.cloned.1.call-update
  530.4 2.4 collective-permute-start
  532.7 0.0 copy-done
  532.8 4.9 collective-permute-start.1
  537.7 1.6 fusion.8
  539.2 0.0 copy-start.1
  539.2 0.0 collective-permute-done
  539.3 1.6 copy-done.1
  540.8 0.0 slice-start
  540.8 2.9 add_convert_fusion
  543.7 0.0 collective-permute-done.1
  543.7 0.0 slice-done
  543.7 2.9 fusion.17
  546.6 128.2 %reduce-scatter.2.cloned.1.call-done = f32[32,1024]{1,0:T(8,128)} async-done(((f32[1024,1024]{1,0:T(8,128)}), f32[32,1024]{1,0:T(8,128)}) %reduce-scatter.2.cloned.1.call-update) | async-done | bytes 131088 | tf_op jit(solution)/shard_map/reduce_scatter | solution.py:52
  (20 shorter events, 0.1 us)
Async XLA Ops:
  7.2 3.3 copy-start.2
  7.2 667.6 %reduce-scatter.2.cloned.1.call-start = ((), (), s32[]{:S(2)}) async-start(), calls=%async_computation.1 | async-start | bytes 4325376 | tf_op jit(solution)/shard_map/reduce_scatter | solution.py:52
  530.3 2.4 copy-start
  530.4 8.9 %collective-permute-start = (bf16[1,128]{1,0:T(2,128)(2,1)S(1)}, bf16[1,128]{1,0:T(2,128)(2,1)S(1)}, u32[]{:S(2)}, u32[]{:S(2)}) collective-permute-start(bf16[1,128]{1,0:T(2,128)(2,1)S(1)} %slice.12), channel_id=1, source_target_pairs={{0,1},{1,2},{2,3},{3,4},{4,5},{5,6},{6,7},{7,8},{8,9},{9,10},{10,1... | collective-permute-start | bytes 776 | tf_op jit(solution)/shard_map/ppermute | solution.py:14
  532.8 11.0 %collective-permute-start.1 = (bf16[1,128,128]{2,1,0:T(8,128)(2,1)S(1)}, bf16[1,128,128]{2,1,0:T(8,128)(2,1)S(1)}, u32[]{:S(2)}, u32[]{:S(2)}) collective-permute-start(bf16[1,128,128]{2,1,0:T(8,128)(2,1)S(1)} %slice.14), channel_id=1, source_target_pairs={{0,1},{1,2},{2,3},{3,4},{4,5},{5,6},{6,7},{7,8},{8,9},{9,10},{10,1... | collective-permute-start | bytes 98312 | tf_op jit(solution)/shard_map/ppermute | solution.py:14
  539.2 1.6 copy-start.1
  540.8 2.9 slice-start
Sparse Core Ops, SparseCore 0:
  530.5 144.2 reduce-scatter.1
where the time goes:
time: 688 us; the launch traced here: 682 us
  other arithmetic  342 us (50%)
  waiting for transfers between devices  128 us (19%)
  local copies, waits for them, and re-layouts  124 us (18%)
  matrix products  66.4 us (10%)
  between operations  14.1 us (2%)
  starting transfers between devices  7.29 us (1%)
    scatter-add x4, other arithmetic, accumulate(): partial_value.at[left_rows, :, right_rows, :]  342 us
    reduce_scatter x1, waiting for transfers between devices, body(): lax.psum_scatter(flat_sum, ('var', 'own', 'sub'), scatter_dimension=0, ti...  128 us
    transpose x4, local copies, waits for them, and re-layouts, accumulate(): jnp.einsum('kpiv,kqjv->kpqij', scaled, blocks, preferred_element_type=jnp...  109 us
    dot_general x4, matrix products, accumulate(): jnp.einsum('kpiv,kqjv->kpqij', scaled, blocks, preferred_element_type=jnp...  59.1 us
  transfers between devices with their start and end apart: 3, of which 1 were waited for; matrix products, arithmetic and copies ran while one was open for 1% of the time, Pallas kernels for 0%

commit v1 on v0

v1 whole, which is shorter than its diff:
```python
import functools

import jax
import jax.numpy as jnp
from jax import lax
from jax.experimental import pallas as pl
from jax.experimental.pallas import tpu as pltpu
from jax.sharding import PartitionSpec as P

CAP = 8
AXES = ("var", "own", "sub")
NT = (((1,), (1,)), ((), ()))
F32, BF16 = jnp.float32, jnp.bfloat16


def swap(value, axis, mask):
    count = lax.axis_size(axis)
    return lax.ppermute(value, axis, [(i, i ^ mask) for i in range(count)])


def shifted(value, axis, steps):
    count = lax.axis_size(axis)
    return lax.ppermute(value, axis, [(i, i + steps) for i in range(count - steps)])


def set_bits(mask, count):
    found = []
    for _ in range(count):
        low = mask & (-mask)
        found.append(
            jnp.where((low & 0xAA) != 0, 1, 0)
            + jnp.where((low & 0xCC) != 0, 2, 0)
            + jnp.where((low & 0xF0) != 0, 4, 0)
        )
        mask = mask ^ low
    return found


def capacity_kernel(step, parts, sizes, rows_ref, place_ref, cap_ref, scale_ref, *rest):
    outs, (dense, scale, acc, sems) = rest[: 2 * len(parts)], rest[2 * len(parts) :]
    count, width = cap_ref.shape[0], cap_ref.shape[2]
    nz = cap_ref.shape[1] // width
    turns = count // step
    side = acc.shape[0]
    tile = 2 * width

    def spot(r):
        return pl.ds(pl.multiple_of(r * width, width), width)

    def issue(k, carry):
        for p in range(nz):
            pltpu.make_async_copy(
                cap_ref.at[k, pl.ds(p * width, width), :],
                dense.at[k, spot(rows_ref[p, k]), :],
                sems.at[k // step],
            ).start()
        return carry

    def clear(k):
        mask = jnp.int32(0)
        for p in range(nz):
            mask = mask | jnp.left_shift(jnp.int32(1), rows_ref[p, k])
        for r in set_bits((1 << CAP) - 1 - mask, CAP - nz):
            dense[k, spot(r), :] = jnp.zeros((width, width), BF16)

    lax.fori_loop(0, step, issue, 0)
    scale[...] = scale_ref[...].astype(F32)
    for k in range(step):
        clear(k)
    lax.fori_loop(step, count, issue, 0)
    acc[...] = jnp.zeros_like(acc)

    def turn(t, carry):
        first = t * step
        pltpu.make_async_copy(
            cap_ref.at[pl.ds(first, step)],
            dense.at[pl.ds(first, step), pl.ds(0, nz * width), :],
            sems.at[t],
        ).wait()
        following = jnp.minimum(t + 1, turns - 1) * step
        for i in range(step):
            clear(following + i)
        ks = [first + i for i in range(step)]
        for j in range(side // tile):
            right = jnp.concatenate(
                [dense[k, pl.ds(tile * j, tile), :] * scale[pl.ds(k, 1), :].astype(BF16) for k in ks], axis=1
            )
            left = jnp.concatenate([dense[k, pl.ds(0, tile * (j + 1)), :] for k in ks], axis=1)
            acc[pl.ds(0, tile * (j + 1)), pl.ds(tile * j, tile)] += lax.dot_general(
                left, right, NT, preferred_element_type=F32
            )
        return carry

    lax.fori_loop(0, turns, turn, 0)
    for i in range(side // tile):
        for j in range(i):
            acc[pl.ds(tile * i, tile), pl.ds(tile * j, tile)] = acc[pl.ds(tile * j, tile), pl.ds(tile * i, tile)].T
    var, own, sub = place_ref[0], place_ref[1], place_ref[2]
    n_var, n_own, held = sizes
    for at, (low, high, order) in enumerate(parts):
        keep_ref, send_ref = outs[2 * at], outs[2 * at + 1]
        for slot, m in enumerate(order):

            def emit(v, carry):
                chip = (var ^ v) * n_own + (own ^ m)
                mine = pl.ds(pl.multiple_of((2 * chip + sub) * held, held), held)
                other = pl.ds(pl.multiple_of((2 * chip + 1 - sub) * held, held), held)
                keep_ref[slot, v] = acc[mine, pl.ds(low, high - low)]
                send_ref[slot, v] = acc[other, pl.ds(low, high - low)].astype(send_ref.dtype)
                return carry

            lax.fori_loop(0, n_var, emit, 0)


def capacity(capacity_blocks, capacity_rows, scaling, parts):
    count, nz, width = capacity_blocks.shape[:3]
    n_var, n_own, n_sub = (lax.axis_size(a) for a in AXES)
    side = CAP * width
    held = side // (n_var * n_own * n_sub)
    step = 16
    place = jnp.stack([lax.axis_index(a) for a in AXES]).astype(jnp.int32)
    sent = BF16 if held % 16 == 0 else F32
    shapes = []
    for low, high, _ in parts:
        shapes += [
            jax.ShapeDtypeStruct((n_own, n_var, held, high - low), F32),
            jax.ShapeDtypeStruct((n_own, n_var, held, high - low), sent),
        ]
    smem, vmem = pl.BlockSpec(memory_space=pltpu.SMEM), pl.BlockSpec(memory_space=pltpu.VMEM)
    flops = 2 * side * side * count * width * 5 // 8
    outs = pl.pallas_call(
        functools.partial(capacity_kernel, step, parts, (n_var, n_own, held)),
        out_shape=shapes,
        in_specs=[smem, smem, pl.BlockSpec(memory_space=pltpu.HBM), vmem],
        out_specs=[vmem] * len(shapes),
        scratch_shapes=[
            pltpu.VMEM((count, side, width), BF16),
            pltpu.VMEM((count, width), F32),
            pltpu.VMEM((side, side), F32),
            pltpu.SemaphoreType.DMA((count // step,)),
        ],
        compiler_params=pltpu.CompilerParams(vmem_limit_bytes=54 * 2**20),
        cost_estimate=pl.CostEstimate(flops=flops, bytes_accessed=14 * 2**20, transcendentals=0),
        name="capacity",
    )(capacity_rows.T, place, capacity_blocks.reshape(count, nz * width, width), scaling)
    return [(keep, send.astype(BF16)) for keep, send in zip(outs[0::2], outs[1::2])]


def cover_kernel(self_ref, before_ref, prev_ref, scale_ref, got_self_ref, got_scale_ref, diag_ref, lower_ref, scale):
    group = self_ref.shape[0]
    at = pl.program_id(0)

    @pl.when(at == 0)
    def _():
        scale[pl.ds(0, 1), :] = got_scale_ref[...].astype(F32)
        scale[pl.ds(8, scale_ref.shape[0]), :] = scale_ref[...].astype(F32)

    base = 8 + at * group
    for k in range(group):
        mine = self_ref[k]
        prev = prev_ref[k]
        if k == 0:
            before = jnp.where(at == 0, got_self_ref[0], before_ref[0])
            scale_before = scale[pl.ds(jnp.where(at == 0, 0, base - 1), 1), :]
        else:
            before = self_ref[k - 1]
            scale_before = scale[pl.ds(base + k - 1, 1), :]
        left = jnp.concatenate(
            [mine * scale[pl.ds(base + k, 1), :].astype(BF16), prev * scale_before.astype(BF16)], axis=1
        )
        right = jnp.concatenate(
            [
                jnp.concatenate([mine, prev], axis=1),
                jnp.concatenate([jnp.zeros_like(before), before], axis=1),
            ],
            axis=0,
        )
        both = lax.dot_general(left, right, NT, preferred_element_type=F32)
        width = mine.shape[0]
        diag_ref[k] = both[:, :width].astype(BF16)
        lower_ref[k] = both[:, width:].astype(BF16)


def cover(cover_self, cover_prev, scaling, got_self, got_scale):
    count, width = cover_self.shape[:2]
    group = 16
    block = pl.BlockSpec((group, width, width), lambda i: (i, 0, 0))
    whole = pl.BlockSpec(memory_space=pltpu.VMEM)
    return pl.pallas_call(
        cover_kernel,
        grid=(count // group,),
        out_shape=[jax.ShapeDtypeStruct(cover_self.shape, BF16)] * 2,
        in_specs=[
            block,
            pl.BlockSpec((1, width, width), lambda i: (jnp.maximum(i * group - 1, 0), 0, 0)),
            block,
            whole,
            whole,
            whole,
        ],
        out_specs=[block, block],
        scratch_shapes=[pltpu.VMEM((8 + count, width), F32)],
        compiler_params=pltpu.CompilerParams(vmem_limit_bytes=16 * 2**20),
        cost_estimate=pl.CostEstimate(
            flops=2 * count * width * 4 * width * width, bytes_accessed=4 * 2 * count * width * width, transcendentals=0
        ),
        name="cover",
    )(cover_self, cover_self, cover_prev, scaling, got_self, got_scale)


def body(capacity_blocks, capacity_rows, cover_self, cover_prev, scaling):
    n_var, n_own, n_sub = (lax.axis_size(a) for a in AXES)
    got_self = shifted(cover_self[-1:], AXES, 1)
    got_scale = shifted(scaling[-1:], AXES, 1)
    side = CAP * capacity_blocks.shape[2]
    ((keep, send),) = capacity(capacity_blocks, capacity_rows, scaling, ((0, side, tuple(range(n_own))),))
    total = keep + swap(send, "sub", 1).astype(F32)
    for axis in ("own", "var"):
        masks = range(1, lax.axis_size(axis))
        arrived = [swap(total[m].astype(BF16), axis, m) for m in masks]
        total = total[0]
        for term in arrived:
            total = total + term.astype(F32)
    diag, lower = cover(cover_self, cover_prev, scaling, got_self, got_scale)
    return (diag, lower, total)


def solution(mesh):
    split = P(AXES)
    return jax.shard_map(
        body, mesh=mesh, in_specs=(split,) * 5, out_specs=(split,) * 3, check_vma=False
    )
```

time: 688 us -> 53.9 us (0.08)
  other arithmetic: 342 us -> 3.59 us
  local copies, waits for them, and re-layouts: 124 us -> 0.09 us
  waiting for transfers between devices: 128 us -> 10.3 us
  matrix products: 66.4 us -> 0 us
  Pallas kernels: 0 us -> 23.4 us
  between operations: 14.1 us -> 0.74 us
  starting transfers between devices: 7.29 us -> 15.4 us
    scatter-add x4 -> x0, other arithmetic: 342 us -> none  [accumulate(): partial_value.at[left_rows, :, right_rows, :]]
    reduce_scatter x1 -> x0, waiting for transfers between devices: 128 us -> none  [body(): lax.psum_scatter(flat_sum, ('var', 'own', 'sub'), scatter_dimension=0, ti...]
    transpose x4 -> x0, local copies, waits for them, and re-layouts: 109 us -> none  [accumulate(): jnp.einsum('kpiv,kqjv->kpqij', scaled, blocks, preferred_element_type=jnp...]
    dot_general x7 -> x0, matrix products: 66.4 us -> none  [the longest x4 59.1 us: accumulate(): jnp.einsum('kpiv,kqjv->kpqij', scaled, blocks, preferred_element_type=jnp...]
    pallas_call x0 -> x2, Pallas kernels: none -> 23.4 us  [the longest x1 18.9 us: capacity(): pl.pallas_call(functools.partial(capacity_kernel, step, parts, (n_var, n_...]
    ppermute x2 -> x9, waiting for transfers between devices: 0.01 us -> 10.3 us  [the longest x7 10.3 us: swap(): return lax.ppermute(value, axis, [(i, i ^ mask) for i in range(count)])]
    ppermute x2 -> x9, starting transfers between devices: 7.25 us -> 15.4 us  [the longest x7 9.57 us: swap(): return lax.ppermute(value, axis, [(i, i ^ mask) for i in range(count)])]
  transfers between devices with their start and end apart: 3 -> 9, of which waited for: 1 -> 3; matrix products, arithmetic and copies ran while one was open for 1% -> 0% of each run, Pallas kernels for 0% -> 8%
where the time goes in v1:
time: 53.9 us; the launch traced here: 53.6 us
  Pallas kernels  23.4 us (43%)
  starting transfers between devices  15.4 us (29%)
  waiting for transfers between devices  10.3 us (19%)
  other arithmetic  3.59 us (7%)
  between operations  0.74 us (1%)
    pallas_call x1, Pallas kernels, capacity(): pl.pallas_call(functools.partial(capacity_kernel, step, parts, (n_var, n_...  18.9 us
    ppermute x7, waiting for transfers between devices, swap(): return lax.ppermute(value, axis, [(i, i ^ mask) for i in range(count)])  10.3 us
    ppermute x7, starting transfers between devices, swap(): return lax.ppermute(value, axis, [(i, i ^ mask) for i in range(count)])  9.57 us
    ppermute x2, starting transfers between devices, shifted(): lax.ppermute(value, axis, [(i, i + steps) for i in range(count - steps)])  5.86 us
    pallas_call x1, Pallas kernels, cover(): pl.pallas_call(cover_kernel, grid=(count // group,), out_shape=[jax.Shape...  4.47 us
    another operation x2, other arithmetic  2.35 us
  transfers between devices with their start and end apart: 9, of which 3 were waited for; matrix products, arithmetic and copies ran while one was open for 0% of the time, Pallas kernels for 8%

profile of v1, /device:TPU:0, one launch (start us, length us, event | category | flops | bytes accessed | tf_op | source)
XLA Modules:
  0.0 53.6 jit_solution(9866493270313575756)
XLA Ops:
  0.6 0.6 %pad_add_fusion.place_ref = s32[3]{0:T(128)} fusion(s32[1]{0:T(128)} %bitcast.3, s32[1]{0:T(128)} %bitcast.2, s32[1]{0:T(128)} %bitcast.1), kind=kLoop, calls=%fused_computation.15 | loop fusion | flops 6 | bytes 24 | tf_op jit(solution)/shard_map/stack | solution.py:121
  1.2 18.9 %capacity.1 = (f32[4,4,32,1024]{3,2,1,0:T(8,128)}, bf16[4,4,32,1024]{3,2,1,0:T(8,128)(2,1)}) custom-call(s32[5,64]{1,0:T(8,128)} %bitcast.35, s32[3]{0:T(128)} %pad_add_fusion.place_ref, bf16[64,640,128]{2,1,0:T(8,128)(2,1)} %bitcast.34, bf16[64,128]{1,0:T(8,128)(2,1)} %scale_ref.3), custom_call_target="tpu_custom_call" | custom-call | flops 10737418240 | bytes 14680064 | tf_op jit(solution)/shard_map/capacity/pallas_call | solution.py:131
  20.1 0.5 collective-permute-start.2
  20.7 2.5 %collective-permute-done.2 = bf16[4,4,32,1024]{3,2,1,0:T(8,128)(2,1)S(1)} collective-permute-done((bf16[4,4,32,1024]{3,2,1,0:T(8,128)(2,1)}, bf16[4,4,32,1024]{3,2,1,0:T(8,128)(2,1)S(1)}, u32[]{:S(2)}, u32[]{:S(2)}) %collective-permute-start.2) | collective-permute-done | bytes 1048608 | tf_op jit(solution)/shard_map/ppermute | solution.py:18
  23.1 0.0 copy-start
  23.2 0.0 copy-start.2
  23.2 2.2 %fusion.8 = (bf16[4,4,32,1024]{3,2,1,0:T(8,128)(2,1)S(1)}, f32[4,4,32,1024]{3,2,1,0:T(8,128)S(1)}) fusion(f32[4,4,32,1024]{3,2,1,0:T(8,128)} %get-tuple-element.9, bf16[4,4,32,1024]{3,2,1,0:T(8,128)(2,1)S(1)} %collective-permute-done.2), kind=kLoop, calls=%fused_computation.17 | loop fusion | flops 1572864 | bytes 6291456 | tf_op jit(solution)/shard_map/convert.5
  25.4 0.0 copy-start.1
  25.4 0.1 slice_bitcast_fusion.3
  25.4 2.9 %collective-permute-start.3 = (bf16[4,32,1024]{2,1,0:T(8,128)(2,1)S(1)}, bf16[4,32,1024]{2,1,0:T(8,128)(2,1)S(1)}, u32[]{:S(2)}, u32[]{:S(2)}) collective-permute-start(bf16[4,32,1024]{2,1,0:T(8,128)(2,1)S(1)} %get-tuple-element.15), channel_id=1, source_target_pairs={{0,2},{2,0},{4,6},{6,4},{1,3},{3,1},{5,7},{7,5},{8,10},{10,8},{12,... | collective-permute-start | bytes 786440 | tf_op jit(solution)/shard_map/ppermute | solution.py:18
  28.4 1.5 %collective-permute-start.4 = (bf16[4,32,1024]{2,1,0:T(8,128)(2,1)S(1)}, bf16[4,32,1024]{2,1,0:T(8,128)(2,1)S(1)}, u32[]{:S(2)}, u32[]{:S(2)}) collective-permute-start(bf16[4,32,1024]{2,1,0:T(8,128)(2,1)S(1)} %get-tuple-element.17), channel_id=1, source_target_pairs={{0,4},{2,6},{4,0},{6,2},{1,5},{3,7},{5,1},{7,3},{8,12},{10,14},{12... | collective-permute-start | bytes 786440 | tf_op jit(solution)/shard_map/ppermute | solution.py:18
  29.9 0.0 collective-permute-start.5
  29.9 0.0 copy-done
  29.9 1.5 %collective-permute-start = (bf16[1,128,128]{2,1,0:T(8,128)(2,1)S(1)}, bf16[1,128,128]{2,1,0:T(8,128)(2,1)S(1)}, u32[]{:S(2)}, u32[]{:S(2)}) collective-permute-start(bf16[1,128,128]{2,1,0:T(8,128)(2,1)S(1)} %slice.36), channel_id=1, source_target_pairs={{0,1},{1,2},{2,3},{3,4},{4,5},{5,6},{6,7},{7,8},{8,9},{9,10},{10,1... | collective-permute-start | bytes 98312 | tf_op jit(solution)/shard_map/ppermute | solution.py:23
  31.4 0.0 copy-done.2
  31.4 4.4 %collective-permute-start.1 = (bf16[1,128]{1,0:T(2,128)(2,1)S(1)}, bf16[1,128]{1,0:T(2,128)(2,1)S(1)}, u32[]{:S(2)}, u32[]{:S(2)}) collective-permute-start(bf16[1,128]{1,0:T(2,128)(2,1)S(1)} %slice.37), channel_id=1, source_target_pairs={{0,1},{1,2},{2,3},{3,4},{4,5},{5,6},{6,7},{7,8},{8,9},{9,10},{10,1... | collective-permute-start | bytes 776 | tf_op jit(solution)/shard_map/ppermute | solution.py:23
  35.8 0.0 collective-permute-done.3
  35.8 6.2 %collective-permute-done.4 = bf16[4,32,1024]{2,1,0:T(8,128)(2,1)S(1)} collective-permute-done((bf16[4,32,1024]{2,1,0:T(8,128)(2,1)S(1)}, bf16[4,32,1024]{2,1,0:T(8,128)(2,1)S(1)}, u32[]{:S(2)}, u32[]{:S(2)}) %collective-permute-start.4) | collective-permute-done | bytes 262176 | tf_op jit(solution)/shard_map/ppermute | solution.py:18
  42.0 0.0 collective-permute-done.5
  42.0 0.2 fusion.6
  42.2 2.0 %collective-permute-start.6 = (bf16[32,1024]{1,0:T(8,128)(2,1)S(1)}, bf16[32,1024]{1,0:T(8,128)(2,1)S(1)}, u32[]{:S(2)}, u32[]{:S(2)}) collective-permute-start(bf16[32,1024]{1,0:T(8,128)(2,1)S(1)} %get-tuple-element.18), channel_id=1, source_target_pairs={{0,8},{8,0},{16,24},{24,16},{1,9},{9,1},{17,25},{25,17},{2,10},{10... | collective-permute-start | bytes 196616 | tf_op jit(solution)/shard_map/ppermute | solution.py:18
  44.2 2.6 %collective-permute-start.7 = (bf16[32,1024]{1,0:T(8,128)(2,1)S(1)}, bf16[32,1024]{1,0:T(8,128)(2,1)S(1)}, u32[]{:S(2)}, u32[]{:S(2)}) collective-permute-start(bf16[32,1024]{1,0:T(8,128)(2,1)S(1)} %get-tuple-element.20), channel_id=1, source_target_pairs={{0,16},{8,24},{16,0},{24,8},{1,17},{9,25},{17,1},{25,9},{2,18},{10... | collective-permute-start | bytes 196616 | tf_op jit(solution)/shard_map/ppermute | solution.py:18
  46.8 0.0 collective-permute-start.8
  46.8 0.0 collective-permute-done.1.got_scale_ref
  46.8 0.0 collective-permute-done.got_self_ref
  46.8 0.0 copy-done.1
  46.9 4.5 %cover.1 = (bf16[64,128,128]{2,1,0:T(8,128)(2,1)}, bf16[64,128,128]{2,1,0:T(8,128)(2,1)}) custom-call(bf16[64,128,128]{2,1,0:T(8,128)(2,1)S(1)} %copy-done, bf16[64,128,128]{2,1,0:T(8,128)(2,1)S(1)} %copy-done, bf16[64,128,128]{2,1,0:T(8,128)(2,1)S(1)} %copy-done.1, bf16[64,128]{1,0:T(8,128)(2,1)S(1)} %copy-done.2, ...), custom_call_target="tpu_custom_call" | custom-call | flops 1073741824 | bytes 8388608 | tf_op jit(solution)/shard_map/cover/pallas_call | solution.py:189
  51.3 0.0 collective-permute-done.6
  51.3 0.0 collective-permute-done.7
  51.3 1.6 %collective-permute-done.8 = bf16[32,1024]{1,0:T(8,128)(2,1)S(1)} collective-permute-done((bf16[32,1024]{1,0:T(8,128)(2,1)S(1)}, bf16[32,1024]{1,0:T(8,128)(2,1)S(1)}, u32[]{:S(2)}, u32[]{:S(2)}) %collective-permute-start.8) | collective-permute-done | bytes 65568 | tf_op jit(solution)/shard_map/ppermute | solution.py:18
  52.9 0.7 %fusion.5 = f32[32,1024]{1,0:T(8,128)} fusion(f32[4,32,1024]{2,1,0:T(8,128)S(1)} %get-tuple-element.12, bf16[32,1024]{1,0:T(8,128)(2,1)S(1)} %collective-permute-done.8, bf16[32,1024]{1,0:T(8,128)(2,1)S(1)} %collective-permute-done.7, bf16[32,1024]{1,0:T(8,128)(2,1)S(1)} %collective-permute-done.6), kind=kLoop, calls=%fused_computation.11 | loop fusion | flops 196608 | bytes 458752 | tf_op jit(solution)/shard_map/add | solution.py:223
  (3 shorter events, 0.0 us)
Async XLA Ops:
  20.1 3.0 %collective-permute-start.2 = (bf16[4,4,32,1024]{3,2,1,0:T(8,128)(2,1)}, bf16[4,4,32,1024]{3,2,1,0:T(8,128)(2,1)S(1)}, u32[]{:S(2)}, u32[]{:S(2)}) collective-permute-start(bf16[4,4,32,1024]{3,2,1,0:T(8,128)(2,1)} %get-tuple-element.10), channel_id=1, source_target_pairs={{0,1},{1,0},{2,3},{3,2},{4,5},{5,4},{6,7},{7,6},{8,9},{9,8},{10,11... | collective-permute-start | bytes 3145736 | tf_op jit(solution)/shard_map/ppermute | solution.py:18
  23.1 6.7 %copy-start = (bf16[64,128,128]{2,1,0:T(8,128)(2,1)S(1)}, bf16[64,128,128]{2,1,0:T(8,128)(2,1)}, u32[]{:S(2)}) copy-start(bf16[64,128,128]{2,1,0:T(8,128)(2,1)} %before_ref.1) | copy-start | bytes 6291460
  23.2 8.2 %copy-start.2 = (bf16[64,128]{1,0:T(8,128)(2,1)S(1)}, bf16[64,128]{1,0:T(8,128)(2,1)}, u32[]{:S(2)}) copy-start(bf16[64,128]{1,0:T(8,128)(2,1)} %scale_ref.3) | copy-start | bytes 49156
  25.4 21.5 %copy-start.1 = (bf16[64,128,128]{2,1,0:T(8,128)(2,1)S(1)}, bf16[64,128,128]{2,1,0:T(8,128)(2,1)}, u32[]{:S(2)}) copy-start(bf16[64,128,128]{2,1,0:T(8,128)(2,1)} %prev_ref.1) | copy-start | bytes 6291460
  25.4 10.4 %collective-permute-start.3 = (bf16[4,32,1024]{2,1,0:T(8,128)(2,1)S(1)}, bf16[4,32,1024]{2,1,0:T(8,128)(2,1)S(1)}, u32[]{:S(2)}, u32[]{:S(2)}) collective-permute-start(bf16[4,32,1024]{2,1,0:T(8,128)(2,1)S(1)} %get-tuple-element.15), channel_id=1, source_target_pairs={{0,2},{2,0},{4,6},{6,4},{1,3},{3,1},{5,7},{7,5},{8,10},{10,8},{12,... | collective-permute-start | bytes 786440 | tf_op jit(solution)/shard_map/ppermute | solution.py:18
  28.4 13.7 %collective-permute-start.4 = (bf16[4,32,1024]{2,1,0:T(8,128)(2,1)S(1)}, bf16[4,32,1024]{2,1,0:T(8,128)(2,1)S(1)}, u32[]{:S(2)}, u32[]{:S(2)}) collective-permute-start(bf16[4,32,1024]{2,1,0:T(8,128)(2,1)S(1)} %get-tuple-element.17), channel_id=1, source_target_pairs={{0,4},{2,6},{4,0},{6,2},{1,5},{3,7},{5,1},{7,3},{8,12},{10,14},{12... | collective-permute-start | bytes 786440 | tf_op jit(solution)/shard_map/ppermute | solution.py:18
  29.9 12.2 %collective-permute-start.5 = (bf16[4,32,1024]{2,1,0:T(8,128)(2,1)S(1)}, bf16[4,32,1024]{2,1,0:T(8,128)(2,1)S(1)}, u32[]{:S(2)}, u32[]{:S(2)}) collective-permute-start(bf16[4,32,1024]{2,1,0:T(8,128)(2,1)S(1)} %get-tuple-element.16), channel_id=1, source_target_pairs={{0,6},{2,4},{4,2},{6,0},{1,7},{3,5},{5,3},{7,1},{8,14},{10,12},{12... | collective-permute-start | bytes 786440 | tf_op jit(solution)/shard_map/ppermute | solution.py:18
  29.9 16.9 %collective-permute-start = (bf16[1,128,128]{2,1,0:T(8,128)(2,1)S(1)}, bf16[1,128,128]{2,1,0:T(8,128)(2,1)S(1)}, u32[]{:S(2)}, u32[]{:S(2)}) collective-permute-start(bf16[1,128,128]{2,1,0:T(8,128)(2,1)S(1)} %slice.36), channel_id=1, source_target_pairs={{0,1},{1,2},{2,3},{3,4},{4,5},{5,6},{6,7},{7,8},{8,9},{9,10},{10,1... | collective-permute-start | bytes 98312 | tf_op jit(solution)/shard_map/ppermute | solution.py:23
  31.4 15.4 %collective-permute-start.1 = (bf16[1,128]{1,0:T(2,128)(2,1)S(1)}, bf16[1,128]{1,0:T(2,128)(2,1)S(1)}, u32[]{:S(2)}, u32[]{:S(2)}) collective-permute-start(bf16[1,128]{1,0:T(2,128)(2,1)S(1)} %slice.37), channel_id=1, source_target_pairs={{0,1},{1,2},{2,3},{3,4},{4,5},{5,6},{6,7},{7,8},{8,9},{9,10},{10,1... | collective-permute-start | bytes 776 | tf_op jit(solution)/shard_map/ppermute | solution.py:23
  42.2 9.1 %collective-permute-start.6 = (bf16[32,1024]{1,0:T(8,128)(2,1)S(1)}, bf16[32,1024]{1,0:T(8,128)(2,1)S(1)}, u32[]{:S(2)}, u32[]{:S(2)}) collective-permute-start(bf16[32,1024]{1,0:T(8,128)(2,1)S(1)} %get-tuple-element.18), channel_id=1, source_target_pairs={{0,8},{8,0},{16,24},{24,16},{1,9},{9,1},{17,25},{25,17},{2,10},{10... | collective-permute-start | bytes 196616 | tf_op jit(solution)/shard_map/ppermute | solution.py:18
  44.2 7.1 %collective-permute-start.7 = (bf16[32,1024]{1,0:T(8,128)(2,1)S(1)}, bf16[32,1024]{1,0:T(8,128)(2,1)S(1)}, u32[]{:S(2)}, u32[]{:S(2)}) collective-permute-start(bf16[32,1024]{1,0:T(8,128)(2,1)S(1)} %get-tuple-element.20), channel_id=1, source_target_pairs={{0,16},{8,24},{16,0},{24,8},{1,17},{9,25},{17,1},{25,9},{2,18},{10... | collective-permute-start | bytes 196616 | tf_op jit(solution)/shard_map/ppermute | solution.py:18
  46.8 6.1 %collective-permute-start.8 = (bf16[32,1024]{1,0:T(8,128)(2,1)S(1)}, bf16[32,1024]{1,0:T(8,128)(2,1)S(1)}, u32[]{:S(2)}, u32[]{:S(2)}) collective-permute-start(bf16[32,1024]{1,0:T(8,128)(2,1)S(1)} %get-tuple-element.19), channel_id=1, source_target_pairs={{0,24},{8,16},{16,8},{24,0},{1,25},{9,17},{17,9},{25,1},{2,26},{10... | collective-permute-start | bytes 196616 | tf_op jit(solution)/shard_map/ppermute | solution.py:18
